TPU v7x, 32 devices: a whole 2x2x4 slice. The times are simulated.
32 devices in a mesh: dp: 4 (over z), expert: 4 (over y, core), tensor: 2 (over x).
Axes of the slice: x: 2, y: 2, z: 4, core: 2. Of those that a mesh axis runs over, the one named last changes fastest.
Arguments:
- tokens: bfloat16 [144, 3072], P(('dp', 'expert'), 'tensor'), may hold values from -6 to 6
- cotangent: bfloat16 [144, 3072], P(('dp', 'expert'), 'tensor'), may hold values from -6 to 6
- routes: int32 [144, 4], P(('dp', 'expert')), may hold values from 0 to 15, all different within a row; in each aligned block of 9 rows (0 to 8, 9 to 17, ...) at most 3 rows name the same one
- gate_probs: float32 [144, 4], P(('dp', 'expert')), may hold values from 0.2 to 1
- gate_proj: bfloat16 [16, 3072, 6144], P('expert', 'tensor', 'dp'), may hold values from -0.109375 to 0.109375
- up_proj: bfloat16 [16, 3072, 6144], P('expert', 'tensor', 'dp'), may hold values from -0.109375 to 0.109375
- down_proj: bfloat16 [16, 6144, 3072], P('expert', 'dp', 'tensor'), may hold values from -0.078125 to 0.078125
Outputs:
- mixture_layer_output: bfloat16 [144, 3072], P(('dp', 'expert'), 'tensor')
- input_token_gradient: bfloat16 [144, 3072], P(('dp', 'expert'), 'tensor')
Inputs may be any that keep to these rules, and one draw needn't show every extreme that they name: `routes`: each row names 4 different experts. Among the 9 rows of one device no expert is named more than 3 times, and in every draw some expert is named exactly 3 times by the rows of some device.
All inputs are finite; a program needn't handle non-finite values.
Results may differ from a plain program's by a relative error of at most 0.019.
Values may be sent and summed in bfloat16 or wider, within the bound.
A program may use at most 128 MiB of HBM per device.

v0:
```python
import jax
import jax.numpy as jnp
from jax import lax
from jax.sharding import PartitionSpec as P

EXPERTS = 16
CAP = 3


def slot_tables(routes, gate_probs, num_experts, capacity):
    tok_count = routes.shape[0]
    top_count = routes.shape[1]
    flat_ids = routes.reshape(-1)
    pair_count = flat_ids.shape[0]
    same_expert = (flat_ids[:, None] == flat_ids[None, :]).astype(jnp.int32)
    earlier = (
        lax.broadcasted_iota(jnp.int32, (pair_count, pair_count), 1)
        < lax.broadcasted_iota(jnp.int32, (pair_count, pair_count), 0)
    ).astype(jnp.int32)
    slot_rank = jnp.sum(same_expert * earlier, axis=1)
    target = (flat_ids * capacity + slot_rank).reshape(tok_count, top_count)
    slot_ids = lax.broadcasted_iota(jnp.int32, (num_experts * capacity, tok_count, top_count), 0)
    matches = (slot_ids == target[None]).astype(jnp.float32)
    dispatch_tokens = jnp.sum(matches, axis=2)
    weighted_output_rows = jnp.sum(matches * gate_probs[None], axis=2)
    return (dispatch_tokens, weighted_output_rows)


def glu_terms(gate_activation_rows, up_activation_rows, backward_activation_rows):
    squashed = jax.nn.sigmoid(gate_activation_rows)
    swished = gate_activation_rows * squashed
    hidden = (swished * up_activation_rows).astype(jnp.bfloat16)
    grad_gate = (
        backward_activation_rows
        * up_activation_rows
        * squashed
        * (1.0 + gate_activation_rows * (1.0 - squashed))
    ).astype(jnp.bfloat16)
    grad_up = (backward_activation_rows * swished).astype(jnp.bfloat16)
    return (hidden, grad_gate, grad_up)


def body(tokens, cotangent, routes, gate_probs, gate_proj, up_proj, down_proj):
    quarter_slice = tokens.shape[1]
    local_experts = gate_proj.shape[0]
    groups = lax.axis_size("expert")
    dispatch_tokens, weighted_output_rows = slot_tables(routes, gate_probs, EXPERTS, CAP)
    sent_tokens = jnp.dot(
        dispatch_tokens.astype(jnp.bfloat16), tokens, preferred_element_type=jnp.float32
    ).astype(jnp.bfloat16)
    sent_grads = jnp.dot(
        weighted_output_rows, cotangent.astype(jnp.float32), precision=lax.Precision.HIGHEST
    ).astype(jnp.bfloat16)
    sent_tokens = sent_tokens.reshape(EXPERTS, CAP, quarter_slice)
    sent_grads = sent_grads.reshape(EXPERTS, CAP, quarter_slice)
    got_tokens, got_grads = (
        lax.all_to_all(sent_tokens, "expert", split_axis=0, concat_axis=0, tiled=True),
        lax.all_to_all(sent_grads, "expert", split_axis=0, concat_axis=0, tiled=True),
    )
    got_tokens = got_tokens.reshape(groups, local_experts, CAP, quarter_slice)
    got_grads = got_grads.reshape(groups, local_experts, CAP, quarter_slice)
    row_tokens, row_grads = (
        lax.all_gather(got_tokens, "dp", axis=0, tiled=True),
        lax.all_gather(got_grads, "dp", axis=0, tiled=True),
    )
    gate_part = jnp.einsum(
        "becd,edf->becf", row_tokens, gate_proj, preferred_element_type=jnp.float32
    )
    up_part = jnp.einsum("becd,edf->becf", row_tokens, up_proj, preferred_element_type=jnp.float32)
    back_part = jnp.einsum(
        "becd,efd->becf", row_grads, down_proj, preferred_element_type=jnp.float32
    )
    gate_activation_rows, up_activation_rows, backward_activation_rows = (
        lax.psum(gate_part.astype(jnp.bfloat16), "tensor").astype(jnp.float32),
        lax.psum(up_part.astype(jnp.bfloat16), "tensor").astype(jnp.float32),
        lax.psum(back_part.astype(jnp.bfloat16), "tensor").astype(jnp.float32),
    )
    hidden, grad_gate, grad_up = glu_terms(
        gate_activation_rows, up_activation_rows, backward_activation_rows
    )
    out_rows = lax.psum_scatter(
        jnp.einsum("becf,efd->becd", hidden, down_proj, preferred_element_type=jnp.float32).astype(
            jnp.bfloat16
        ),
        "dp",
        scatter_dimension=0,
        tiled=True,
    ).astype(jnp.float32)
    from_gate = jnp.einsum(
        "becf,edf->becd", grad_gate, gate_proj, preferred_element_type=jnp.float32
    )
    from_up = jnp.einsum("becf,edf->becd", grad_up, up_proj, preferred_element_type=jnp.float32)
    in_rows = lax.psum_scatter(
        (from_gate + from_up).astype(jnp.bfloat16), "dp", scatter_dimension=0, tiled=True
    ).astype(jnp.float32)
    out_rows = out_rows.astype(jnp.bfloat16)
    in_rows = in_rows.astype(jnp.bfloat16)
    back_out, back_in = (
        lax.all_to_all(out_rows, "expert", split_axis=0, concat_axis=0, tiled=True),
        lax.all_to_all(in_rows, "expert", split_axis=0, concat_axis=0, tiled=True),
    )
    flat_out = back_out.reshape(EXPERTS * CAP, quarter_slice).astype(jnp.float32)
    flat_in = back_in.reshape(EXPERTS * CAP, quarter_slice).astype(jnp.float32)
    mixture_layer_output = jnp.dot(
        weighted_output_rows.T, flat_out, precision=lax.Precision.HIGHEST
    ).astype(jnp.bfloat16)
    input_token_gradient = jnp.dot(
        dispatch_tokens.T, flat_in, precision=lax.Precision.HIGHEST
    ).astype(jnp.bfloat16)
    return (mixture_layer_output, input_token_gradient)


def solution(mesh):
    in_specs = (
        P(("dp", "expert"), "tensor"),
        P(("dp", "expert"), "tensor"),
        P(("dp", "expert"), None),
        P(("dp", "expert"), None),
        P("expert", "tensor", "dp"),
        P("expert", "tensor", "dp"),
        P("expert", "dp", "tensor"),
    )
    out_specs = (P(("dp", "expert"), "tensor"), P(("dp", "expert"), "tensor"))
    return jax.shard_map(body, mesh=mesh, in_specs=in_specs, out_specs=out_specs, check_vma=False)
```

profile of v0, /device:TPU:0, one launch (start us, length us, event | category | flops | bytes accessed | tf_op | source)
XLA Modules:
  0.0 256.1 jit_solution(14123434681130172378)
XLA Ops:
  7.2 0.8 copy.47
  8.3 0.8 copy.49
  9.4 0.8 reshape.32
  10.2 4.2 %all-to-all-start = ((bf16[16,3,1536]{2,1,0:T(4,128)(2,1)}), bf16[16,3,1536]{2,1,0:T(4,128)(2,1)S(1)}, u32[]{:S(2)}, u32[]{:S(2)}) async-start(bf16[16,3,1536]{2,1,0:T(4,128)(2,1)} %reshape.32), calls=%async_computation | async-start | bytes 393216 | tf_op jit(solution)/shard_map/all_to_all | solution.py:57
  14.4 1.1 convolution_convert_fusion
  15.6 0.8 reshape.35
  16.3 3.4 %all-to-all-done = bf16[16,3,1536]{2,1,0:T(4,128)(2,1)S(1)} async-done(((bf16[16,3,1536]{2,1,0:T(4,128)(2,1)}), bf16[16,3,1536]{2,1,0:T(4,128)(2,1)S(1)}, u32[]{:S(2)}, u32[]{:S(2)}) %all-to-all-start) | async-done | bytes 147488 | tf_op jit(solution)/shard_map/all_to_all | solution.py:57
  19.8 3.4 %all-to-all-start.2 = ((bf16[16,3,1536]{2,1,0:T(4,128)(2,1)}), bf16[16,3,1536]{2,1,0:T(4,128)(2,1)S(1)}, u32[]{:S(2)}, u32[]{:S(2)}) async-start(bf16[16,3,1536]{2,1,0:T(4,128)(2,1)} %reshape.35), calls=%async_computation.2 | async-start | bytes 393216 | tf_op jit(solution)/shard_map/all_to_all | solution.py:58
  23.3 18.1 %all_gather.6 = bf16[16,4,3,1536]{3,1,2,0:T(4,128)(2,1)S(1)} all-gather(bf16[4,4,3,1536]{3,1,2,0:T(4,128)(2,1)S(1)} %copy.51), channel_id=1, replica_groups=mesh['dp'=4,'expert'=4,'tensor'=2] {'dp'}, dimensions={0}, use_global_device_ids=true | all-gather | bytes 737280 | tf_op jit(solution)/shard_map/all_gather | solution.py:63
  41.4 10.5 %fusion.30 = bf16[16,4,3,1536]{3,0,2,1:T(8,128)(2,1)} fusion(bf16[4,1536,1536]{2,1,0:T(8,128)(2,1)} %param.12, bf16[16,4,3,1536]{3,1,2,0:T(4,128)(2,1)S(1)} %all_gather.6), kind=kOutput, calls=%fused_computation.18 | convolution fusion | flops 906264576 | bytes 20054016 | tf_op jit(solution)/shard_map/becd,edf->becf/dot_general | solution.py:69
  51.9 1.4 copy-done.2
  53.3 4.0 %fusion.33 = bf16[16,4,3,1536]{3,0,2,1:T(8,128)(2,1)} fusion(bf16[4,1536,1536]{2,1,0:T(8,128)(2,1)S(1)} %copy-done.2, bf16[16,4,3,1536]{3,1,2,0:T(4,128)(2,1)S(1)} %all_gather.6), kind=kOutput, calls=%fused_computation.19 | convolution fusion | flops 906264576 | bytes 20054016 | tf_op jit(solution)/shard_map/becd,edf->becf/dot_general | solution.py:66
  57.4 16.1 %all_gather.7 = bf16[16,4,3,1536]{3,1,2,0:T(4,128)(2,1)S(1)} all-gather(bf16[4,4,3,1536]{3,1,2,0:T(4,128)(2,1)S(1)} %copy.57), channel_id=1, replica_groups=mesh['dp'=4,'expert'=4,'tensor'=2] {'dp'}, dimensions={0}, use_global_device_ids=true | all-gather | bytes 737280 | tf_op jit(solution)/shard_map/all_gather | solution.py:64
  73.6 12.8 %fusion.36 = bf16[16,4,3,1536]{3,0,2,1:T(8,128)(2,1)} fusion(bf16[4,1536,1536]{2,1,0:T(8,128)(2,1)} %param.13, bf16[16,4,3,1536]{3,1,2,0:T(4,128)(2,1)S(1)} %all_gather.7), kind=kOutput, calls=%fused_computation.20 | convolution fusion | flops 906264576 | bytes 20054016 | tf_op jit(solution)/shard_map/becd,efd->becf/dot_general | solution.py:70
  86.3 0.2 all-reduce.7.cloned.1.call-start
  86.6 56.4 %all-reduce.9.cloned.1.call-done = (bf16[16,4,3,1536]{3,0,2,1:T(8,128)(2,1)}, bf16[16,4,3,1536]{3,0,2,1:T(8,128)(2,1)}, bf16[16,4,3,1536]{3,0,2,1:T(8,128)(2,1)}) async-done(((bf16[16,4,3,1536]{3,0,2,1:T(8,128)(2,1)}, bf16[16,4,3,1536]{3,0,2,1:T(8,128)(2,1)}, bf16[16,4,3,1536]{3,0,2,1:T(8,128)(2,1)}), (bf16[16,4,3,1536]{3,0,2,1:T(8,128)(2,1)}, bf16[16,4,3,1536]{3,0,2,1:T(8,128)(2,1)}, ...) | async-done | bytes 1769488 | tf_op jit(solution)/shard_map/psum | solution.py:75
  142.9 9.9 %fusion = f32[4,16,3,1536]{3,1,2,0:T(8,128)S(1)} fusion(bf16[4,1536,1536]{2,1,0:T(8,128)(2,1)} %param.12, bf16[16,4,3,1536]{3,0,2,1:T(8,128)(2,1)} %get-tuple-element.8, bf16[16,4,3,1536]{3,0,2,1:T(8,128)(2,1)} %get-tuple-element.7), kind=kOutput, calls=%fused_computation | convolution fusion | flops 908328960 | bytes 21233664 | tf_op jit(solution)/shard_map/becf,edf->becd/dot_general | solution.py:92
  152.9 10.5 %fusion.39 = bf16[16,4,3,1536]{3,0,2,1:T(8,128)(2,1)} fusion(bf16[4,1536,1536]{2,1,0:T(8,128)(2,1)} %param.13, bf16[16,4,3,1536]{3,0,2,1:T(8,128)(2,1)S(1)} %copy-done.5, bf16[16,4,3,1536]{3,0,2,1:T(8,128)(2,1)S(1)} %copy-done.3), kind=kOutput, calls=%fused_computation.21 | convolution fusion | flops 908623872 | bytes 20643840 | tf_op jit(solution)/shard_map/becf,efd->becd/dot_general | solution.py:82
  163.4 10.4 %fusion.42 = bf16[16,4,3,1536]{3,0,2,1:T(8,128)(2,1)} fusion(f32[4,16,3,1536]{3,1,2,0:T(8,128)S(1)} %fusion, bf16[4,1536,1536]{2,1,0:T(8,128)(2,1)} %param.11, bf16[16,4,3,1536]{3,0,2,1:T(8,128)(2,1)S(1)} %copy-done.5, bf16[16,4,3,1536]{3,0,2,1:T(8,128)(2,1)S(1)} %copy-done.4, bf16[16,4,3,1536]{3,0,2,1:T(8,128)(2,1)S(1)} %copy-done.3), kind=kOutput, calls=%fused_computation.22 | convolution fusion | flops 910393344 | bytes 22413312 | tf_op jit(solution)/shard_map/becf,edf->becd/dot_general | solution.py:89
  173.8 0.6 copy-done.6
  174.4 0.6 dynamic-slice
  175.6 54.6 %all-reduce.7.cloned.1.call-done = (bf16[16,4,3,1536]{3,0,2,1:T(8,128)(2,1)}, bf16[16,4,3,1536]{3,0,2,1:T(8,128)(2,1)}) async-done(((bf16[16,4,3,1536]{3,0,2,1:T(8,128)(2,1)}, bf16[16,4,3,1536]{3,0,2,1:T(8,128)(2,1)}), (bf16[16,4,3,1536]{3,0,2,1:T(8,128)(2,1)}, bf16[16,4,3,1536]{3,0,2,1:T(8,128)(2,1)})) %all-reduce.7.cloned.1.call-update) | async-done | bytes 1179664
  230.2 1.0 constant_dynamic-slice_fusion
  231.2 0.7 copy.59
  232.0 3.3 %all-to-all-start.3 = ((bf16[4,4,3,1536]{3,1,2,0:T(4,128)(2,1)}), bf16[4,4,3,1536]{3,1,2,0:T(4,128)(2,1)S(1)}, u32[]{:S(2)}, u32[]{:S(2)}) async-start(bf16[4,4,3,1536]{3,1,2,0:T(4,128)(2,1)} %copy.59), calls=%async_computation.3 | async-start | bytes 294912 | tf_op jit(solution)/shard_map/all_to_all | solution.py:100
  235.3 1.1 constant_dynamic-slice_fusion.1
  236.4 0.7 copy.54
  237.1 3.0 %all-to-all-done.3 = bf16[4,4,3,1536]{3,1,2,0:T(4,128)(2,1)S(1)} async-done(((bf16[4,4,3,1536]{3,1,2,0:T(4,128)(2,1)}), bf16[4,4,3,1536]{3,1,2,0:T(4,128)(2,1)S(1)}, u32[]{:S(2)}, u32[]{:S(2)}) %all-to-all-start.3) | async-done | bytes 147488 | tf_op jit(solution)/shard_map/all_to_all | solution.py:100
  240.1 3.3 %all-to-all-start.1 = ((bf16[4,4,3,1536]{3,1,2,0:T(4,128)(2,1)}), bf16[4,4,3,1536]{3,1,2,0:T(4,128)(2,1)S(1)}, u32[]{:S(2)}, u32[]{:S(2)}) async-start(bf16[4,4,3,1536]{3,1,2,0:T(4,128)(2,1)} %copy.54), calls=%async_computation.1 | async-start | bytes 294912 | tf_op jit(solution)/shard_map/all_to_all | solution.py:99
  243.6 0.8 convolution_convert_fusion.2
  244.5 3.7 %all-to-all-done.1 = bf16[4,4,3,1536]{3,1,2,0:T(4,128)(2,1)S(1)} async-done(((bf16[4,4,3,1536]{3,1,2,0:T(4,128)(2,1)}), bf16[4,4,3,1536]{3,1,2,0:T(4,128)(2,1)S(1)}, u32[]{:S(2)}, u32[]{:S(2)}) %all-to-all-start.1) | async-done | bytes 147488 | tf_op jit(solution)/shard_map/all_to_all | solution.py:99
  248.4 0.8 convolution_convert_fusion.3
  (28 shorter events, 1.3 us)
Async XLA Ops:
  7.2 2.0 copy-start
  10.2 9.6 %all-to-all-start = ((bf16[16,3,1536]{2,1,0:T(4,128)(2,1)}), bf16[16,3,1536]{2,1,0:T(4,128)(2,1)S(1)}, u32[]{:S(2)}, u32[]{:S(2)}) async-start(bf16[16,3,1536]{2,1,0:T(4,128)(2,1)} %reshape.32), calls=%async_computation | async-start | bytes 393216 | tf_op jit(solution)/shard_map/all_to_all | solution.py:57
  19.8 37.6 %all-to-all-start.2 = ((bf16[16,3,1536]{2,1,0:T(4,128)(2,1)}), bf16[16,3,1536]{2,1,0:T(4,128)(2,1)S(1)}, u32[]{:S(2)}, u32[]{:S(2)}) async-start(bf16[16,3,1536]{2,1,0:T(4,128)(2,1)} %reshape.35), calls=%async_computation.2 | async-start | bytes 393216 | tf_op jit(solution)/shard_map/all_to_all | solution.py:58
  23.1 119.8 %all-reduce.9.cloned.1.call-start = ((), (), s32[]{:S(2)}) async-start(), calls=%async_computation.5 | async-start | bytes 3538944 | tf_op jit(solution)/shard_map/psum | solution.py:75
  41.4 11.9 %copy-start.2 = (bf16[4,1536,1536]{2,1,0:T(8,128)(2,1)S(1)}, bf16[4,1536,1536]{2,1,0:T(8,128)(2,1)}, u32[]{:S(2)}) copy-start(bf16[4,1536,1536]{2,1,0:T(8,128)(2,1)} %param.11) | copy-start | bytes 56623108
  86.3 143.9 %all-reduce.7.cloned.1.call-start = ((), (), s32[]{:S(2)}) async-start(), calls=%async_computation.4 | async-start | bytes 2359296
  142.9 9.9 %copy-start.3 = (bf16[16,4,3,1536]{3,0,2,1:T(8,128)(2,1)S(1)}, bf16[16,4,3,1536]{3,0,2,1:T(8,128)(2,1)}, u32[]{:S(2)}) copy-start(bf16[16,4,3,1536]{3,0,2,1:T(8,128)(2,1)} %get-tuple-element.7) | copy-start | bytes 1769476
  142.9 9.9 %copy-start.5 = (bf16[16,4,3,1536]{3,0,2,1:T(8,128)(2,1)S(1)}, bf16[16,4,3,1536]{3,0,2,1:T(8,128)(2,1)}, u32[]{:S(2)}) copy-start(bf16[16,4,3,1536]{3,0,2,1:T(8,128)(2,1)} %get-tuple-element.6) | copy-start | bytes 1769476
  152.8 10.5 %copy-start.4 = (bf16[16,4,3,1536]{3,0,2,1:T(8,128)(2,1)S(1)}, bf16[16,4,3,1536]{3,0,2,1:T(8,128)(2,1)}, u32[]{:S(2)}) copy-start(bf16[16,4,3,1536]{3,0,2,1:T(8,128)(2,1)} %get-tuple-element.8) | copy-start | bytes 1769476
  173.8 0.7 copy-start.6
  232.0 8.1 %all-to-all-start.3 = ((bf16[4,4,3,1536]{3,1,2,0:T(4,128)(2,1)}), bf16[4,4,3,1536]{3,1,2,0:T(4,128)(2,1)S(1)}, u32[]{:S(2)}, u32[]{:S(2)}) async-start(bf16[4,4,3,1536]{3,1,2,0:T(4,128)(2,1)} %copy.59), calls=%async_computation.3 | async-start | bytes 294912 | tf_op jit(solution)/shard_map/all_to_all | solution.py:100
  235.3 13.9 %copy-start.1 = (bf16[9,1536]{1,0:T(8,128)(2,1)S(1)}, bf16[9,1536]{1,0:T(8,128)(2,1)}, u32[]{:S(2)}) copy-start(bf16[9,1536]{1,0:T(8,128)(2,1)} %param.7) | copy-start | bytes 82948
  240.1 8.1 %all-to-all-start.1 = ((bf16[4,4,3,1536]{3,1,2,0:T(4,128)(2,1)}), bf16[4,4,3,1536]{3,1,2,0:T(4,128)(2,1)S(1)}, u32[]{:S(2)}, u32[]{:S(2)}) async-start(bf16[4,4,3,1536]{3,1,2,0:T(4,128)(2,1)} %copy.54), calls=%async_computation.1 | async-start | bytes 294912 | tf_op jit(solution)/shard_map/all_to_all | solution.py:99
Sparse Core Ops, SparseCore 0:
  86.5 56.4 all-reduce.8
  173.9 56.2 all-reduce.6
where the time goes:
time: 257 us; the launch traced here: 256 us
  waiting for transfers between devices  121 us (47%)
  matrix products  61.1 us (24%)
  blocking collectives  34.2 us (13%)
  between operations  14.8 us (6%)
  starting transfers between devices  14.5 us (6%)
  local copies, waits for them, and re-layouts  9.97 us (4%)
    psum x1, waiting for transfers between devices, body(): lax.psum(up_part.astype(jnp.bfloat16), 'tensor').astype(jnp.float32)  56.4 us
    unnamed x3, waiting for transfers between devices  54.6 us
    all_gather x1, blocking collectives, body(): lax.all_gather(got_tokens, 'dp', axis=0, tiled=True)  18.1 us
    all_gather x1, blocking collectives, body(): lax.all_gather(got_grads, 'dp', axis=0, tiled=True)  16.1 us
    dot_general x1, matrix products, body(): jnp.einsum('becd,efd->becf', row_grads, down_proj, preferred_element_type...  12.8 us
    dot_general x1, matrix products, body(): jnp.einsum('becd,edf->becf', row_tokens, up_proj, preferred_element_type=...  10.5 us
    dot_general x1, matrix products, body(): jnp.einsum('becf,efd->becd', hidden, down_proj, preferred_element_type=jn...  10.5 us
    dot_general x1, matrix products, body(): jnp.einsum('becf,edf->becd', grad_gate, gate_proj, preferred_element_type...  10.4 us
  transfers between devices with their start and end apart: 6, of which 5 were waited for; matrix products, arithmetic and copies ran while one was open for 8% of the time, Pallas kernels for 0%

commit v1 on v0

--- a/solution.py
+++ b/solution.py
@@ -1,10 +1,13 @@
 import jax
 import jax.numpy as jnp
 from jax import lax
+from jax.experimental import pallas as pl
+from jax.experimental.pallas import tpu as pltpu
 from jax.sharding import PartitionSpec as P
 
 EXPERTS = 16
 CAP = 3
+VMEM_BYTES = 67000000
 
 
 def slot_tables(routes, gate_probs, num_experts, capacity):
@@ -110,6 +113,321 @@
     return (mixture_layer_output, input_token_gradient)
 
 
+PACK = 16
+CHUNK = 256
+
+
+def packed_rows(first, second):
+    width = first.shape[1]
+    split = PACK - first.shape[0]
+    pieces = second[split:].reshape(-1, CHUNK)
+    pieces = jnp.pad(pieces, ((0, PACK - pieces.shape[0]), (0, 0)))
+    return jnp.concatenate([jnp.concatenate([first, second[:split]], axis=0), pieces], axis=1)
+
+
+def unpacked_rows(packed, count):
+    width = packed.shape[1] - CHUNK
+    split = PACK - count
+    pieces = (count - split) * width // CHUNK
+    tail = packed[:pieces, width:].reshape(count - split, width)
+    return packed[:count, :width], jnp.concatenate([packed[count:, :width], tail], axis=0)
+
+
+def routing_table(routes, gate_probs, place, blocks, groups):
+    count = routes.shape[0]
+    local = EXPERTS // groups
+    same = routes[None] == jnp.arange(EXPERTS)[:, None, None]
+    hit = jnp.any(same, axis=2)
+    prob = jnp.sum(jnp.where(same, gate_probs[None], 0.0), axis=2)
+    before = jnp.arange(count)[None, :] < jnp.arange(count)[:, None]
+    rank = jnp.sum(hit[:, None, :] & before[None], axis=2)
+    mine = hit[:, None, :] & (rank[:, None, :] == jnp.arange(CAP)[None, :, None])
+    rows = (place * PACK + 1 + jnp.arange(count)).astype(jnp.float32)
+    token = jnp.sum(jnp.where(mine, rows[None, None], 0.0), axis=2)
+    weight = jnp.sum(jnp.where(mine, prob[:, None, :], 0.0), axis=2)
+    both = jnp.stack([token, weight]).reshape(2 * groups, local, 1, CAP)
+    here = (jnp.arange(blocks) == place)[None, None, :, None]
+    table = jnp.where(here, both, 0.0).reshape(2 * groups, local * blocks * CAP)
+    return jnp.pad(table, ((0, 0), (0, 256 - table.shape[1])))
+
+
+def nt_dot(a, b):
+    return lax.dot_general(a, b, (((1,), (1,)), ((), ())), preferred_element_type=jnp.float32)
+
+
+def nn_dot(a, b):
+    return jnp.dot(a, b, preferred_element_type=jnp.float32)
+
+
+def glu_kernel(
+    x_ref, t_ref, wg_hbm, wu_hbm, wd_hbm, o_ref,
+    w_v, gb, tab, xt, xg, pc, sbuf, rbuf, act, p_in, p_out, r1, s2, r2, s3, r3,
+    w_sem, g_ss, g_rs, x_ss, x_rs, e_ss, e_rs,
+):
+    f32, bf16 = jnp.float32, jnp.bfloat16
+    width = x_ref.shape[1] - CHUNK
+    local, hidden_width = wg_hbm.shape[0], wg_hbm.shape[2]
+    rows = sbuf.shape[2]
+    slots = local * rows
+    n_dp = lax.axis_size("dp")
+    z, e, t = lax.axis_index("dp"), lax.axis_index("expert"), lax.axis_index("tensor")
+    across = lax.rem(e + 2, 4)
+    beside = e + 1 - 2 * lax.rem(e, 2)
+    diagonal = lax.rem(beside + 2, 4)
+    other = 1 - t
+    span = n_dp * PACK
+
+    hbm = (wg_hbm, wu_hbm, wd_hbm)
+
+    def weight(m, j):
+        return pltpu.make_async_copy(hbm[m].at[j], w_v.at[m, j], w_sem.at[m, j])
+
+    def remote(src, dst, ss, rs, i, where):
+        return pltpu.make_async_remote_copy(
+            src_ref=src, dst_ref=dst, send_sem=ss.at[i], recv_sem=rs.at[i],
+            device_id=where, device_id_type=pl.DeviceIdType.MESH,
+        )
+
+    def at_rows(k, n):
+        return pl.ds(pl.multiple_of(k, PACK), n)
+
+    barrier = pltpu.get_barrier_semaphore()
+    partners = [{"dp": lax.rem(z + d, n_dp)} for d in range(1, n_dp)]
+    partners += [{"expert": across}, {"expert": beside}, {"tensor": other}]
+    for p in partners:
+        pl.semaphore_signal(barrier, inc=1, device_id=p, device_id_type=pl.DeviceIdType.MESH)
+    for j in range(local):
+        for m in range(3):
+            weight(m, j).start()
+    place = e * n_dp + z
+    own = at_rows(place * PACK, PACK)
+    gb[own, :] = x_ref[...]
+    tab[pl.ds(place, 1)] = t_ref[...][None]
+    p_in[slots:, :] = jnp.zeros((p_in.shape[0] - slots, width), bf16)
+    p_out[slots:, :] = jnp.zeros((p_out.shape[0] - slots, width), bf16)
+    pl.semaphore_wait(barrier, len(partners))
+
+    first = []
+    for d in range(1, n_dp):
+        to = {"dp": lax.rem(z + d, n_dp)}
+        first.append(remote(gb.at[own], gb.at[own], g_ss, g_rs, 2 * d - 2, to))
+        first.append(
+            remote(tab.at[pl.ds(place, 1)], tab.at[pl.ds(place, 1)], g_ss, g_rs, 2 * d - 1, to)
+        )
+    for c in first:
+        c.start()
+    for c in first:
+        c.wait_recv()
+
+    def send_group(k, group, to):
+        a = at_rows(group * span, span)
+        b = pl.ds(group * n_dp, n_dp)
+        pair = [
+            remote(gb.at[a], gb.at[a], g_ss, g_rs, k, to),
+            remote(tab.at[b], tab.at[b], g_ss, g_rs, k + 1, to),
+        ]
+        for c in pair:
+            c.start()
+        return pair
+
+    second = send_group(6, e, {"expert": across})
+    third = send_group(8, e, {"expert": beside})
+    for c in second:
+        c.wait_recv()
+    fourth = send_group(10, across, {"expert": beside})
+    for c in third + fourth:
+        c.wait_recv()
+
+    row_of = jnp.sum(tab[:, pl.ds(e, 1), :], axis=0)
+    prob_of = jnp.sum(tab[:, pl.ds(e + 4, 1), :], axis=0)
+
+    def keys(v):
+        k = v - 1.0
+        base = jnp.floor(k * (1.0 / PACK)) * PACK
+        r = k - base
+        tokens_count = 9.0
+        split = PACK - tokens_count
+        second_key = jnp.where(r < split, k + tokens_count, -1.0)
+        tail_key = jnp.where(
+            (r >= split) & (r < tokens_count), base + (r - split) * (width // CHUNK), -1000.0
+        )
+        return k.astype(jnp.int32), second_key.astype(jnp.int32), tail_key.astype(jnp.int32)
+
+    def one_hot(hit):
+        return jnp.where(hit, 1.0, 0.0).astype(bf16)
+
+    column = jnp.transpose(jnp.broadcast_to(row_of, (128, row_of.shape[1])))[:slots]
+    pc[...] = jnp.transpose(jnp.broadcast_to(prob_of, (128, prob_of.shape[1])))[:slots]
+    wide = jnp.concatenate([column, column], axis=1)
+    k1, k2, k3 = keys(wide)
+    lane = lax.broadcasted_iota(jnp.int32, (slots, 256), 1)
+    pick_first, pick_second = one_hot(k1 == lane), one_hot(k2 == lane)
+    scale = pc[:, 0:1]
+    for q in range(width // CHUNK):
+        cols = pl.ds(q * CHUNK, CHUNK)
+        xt[:, cols] = nn_dot(pick_first, gb[:, cols]).astype(bf16)
+        g = nn_dot(pick_second, gb[:, cols])
+        g += nn_dot(one_hot(k3 + q == lane), gb[:, width:])
+        xg[:, cols] = (scale * g).astype(bf16)
+
+    def act_copy(j, m):
+        return pltpu.make_async_remote_copy(
+            src_ref=sbuf.at[j, m], dst_ref=rbuf.at[j, m],
+            send_sem=x_ss.at[j, m], recv_sem=x_rs.at[j, m],
+            device_id={"tensor": other}, device_id_type=pl.DeviceIdType.MESH,
+        )
+
+    def project(j, carry):
+        mine = at_rows(j * rows, rows)
+        for m in range(3):
+            weight(m, j).wait()
+
+            def tile(n, c):
+                cols = pl.ds(pl.multiple_of(n * CHUNK, CHUNK), CHUNK)
+                if m < 2:
+                    part = nn_dot(xt[mine, :], w_v[m, j, :, cols])
+                else:
+                    part = nt_dot(xg[mine, :], w_v[m, j, cols, :])
+                sbuf[j, m, :, cols] = part.astype(bf16)
+                return c
+
+            lax.fori_loop(0, hidden_width // CHUNK, tile, 0)
+            act_copy(j, m).start()
+        return carry
+
+    lax.fori_loop(0, local, project, 0)
+
+    def finish(j, carry):
+        mine = at_rows(j * rows, rows)
+        for m in range(3):
+            act_copy(j, m).wait_recv()
+
+        def terms(n, c):
+            cols = pl.ds(pl.multiple_of(n * CHUNK, CHUNK), CHUNK)
+            total = [
+                sbuf[j, m, :, cols].astype(f32) + rbuf[j, m, :, cols].astype(f32) for m in range(3)
+            ]
+            for m, v in enumerate(glu_terms(*total)):
+                act[m, :, cols] = v
+            return c
+
+        lax.fori_loop(0, hidden_width // CHUNK, terms, 0)
+        by = pc[mine, 0:1]
+
+        def tile(n, c):
+            cols = pl.ds(pl.multiple_of(n * CHUNK, CHUNK), CHUNK)
+            out = nn_dot(act[0], w_v[2, j, :, cols])
+            p_out[mine, cols] = (by * out).astype(bf16)
+            back = nt_dot(act[1], w_v[0, j, cols, :]) + nt_dot(act[2], w_v[1, j, cols, :])
+            p_in[mine, cols] = back.astype(bf16)
+            return c
+
+        lax.fori_loop(0, width // CHUNK, tile, 0)
+        return carry
+
+    lax.fori_loop(0, local, finish, 0)
+
+    for c in first + second + third + fourth:
+        c.wait_send()
+    acc = gb
+    n1, n2, n3 = keys(row_of)
+    down = lax.broadcasted_iota(jnp.int32, (gb.shape[0], row_of.shape[1]), 0)
+    put_first, put_second = one_hot(n1 == down), one_hot(n2 == down)
+    tail = jnp.zeros((gb.shape[0], CHUNK), f32)
+    for q in range(width // CHUNK):
+        cols = pl.ds(q * CHUNK, CHUNK)
+        v = nn_dot(put_first, p_in[:, cols]) + nn_dot(put_second, p_out[:, cols])
+        acc[:, cols] = v.astype(bf16)
+        tail += nn_dot(one_hot(n3 + q == down), p_out[:, cols])
+    acc[:, width:] = tail.astype(bf16)
+
+    a1 = remote(acc.at[at_rows(diagonal * span, span)], r1.at[1], e_ss, e_rs, 0, {"expert": beside})
+    a0 = remote(acc.at[at_rows(beside * span, span)], r1.at[0], e_ss, e_rs, 1, {"expert": beside})
+    a1.start()
+    a0.start()
+    a1.wait_recv()
+    s2[...] = (acc[at_rows(across * span, span), :].astype(f32) + r1[1].astype(f32)).astype(bf16)
+    b = remote(s2, r2, e_ss, e_rs, 2, {"expert": across})
+    b.start()
+    a0.wait_recv()
+    held = acc[at_rows(e * span, span), :].astype(f32) + r1[0].astype(f32)
+    b.wait_recv()
+    s3[...] = (held + r2[...].astype(f32)).astype(bf16)
+    last = []
+    for d in range(1, n_dp):
+        to = lax.rem(z + d, n_dp)
+        c = remote(
+            s3.at[at_rows(to * PACK, PACK)], r3.at[d - 1], e_ss, e_rs, 2 + d, {"dp": to}
+        )
+        c.start()
+        last.append(c)
+    final = s3[at_rows(z * PACK, PACK), :].astype(f32)
+    for d, c in enumerate(last):
+        c.wait_recv()
+        final += r3[d].astype(f32)
+    o_ref[...] = final.astype(bf16)
+
+    for c in [a1, a0, b] + last:
+        c.wait_send()
+
+    def sent(j, carry):
+        for m in range(3):
+            act_copy(j, m).wait_send()
+        return carry
+
+    lax.fori_loop(0, local, sent, 0)
+
+
+def kernel_body(tokens, cotangent, routes, gate_probs, gate_proj, up_proj, down_proj):
+    groups, n_dp = lax.axis_size("expert"), lax.axis_size("dp")
+    blocks = groups * n_dp
+    place = lax.axis_index("expert") * n_dp + lax.axis_index("dp")
+    count, width = tokens.shape
+    local, _, hidden_width = gate_proj.shape
+    rows = blocks * CAP
+    packed = packed_rows(tokens, cotangent)
+    table = routing_table(routes, gate_probs, place, blocks, groups)
+    bf16, dma = jnp.bfloat16, pltpu.SemaphoreType.DMA
+    full, span = width + CHUNK, n_dp * PACK
+    out = pl.pallas_call(
+        glu_kernel,
+        out_shape=jax.ShapeDtypeStruct((PACK, full), bf16),
+        in_specs=[pl.BlockSpec(memory_space=pltpu.VMEM)] * 2
+        + [pl.BlockSpec(memory_space=pl.ANY)] * 3,
+        out_specs=pl.BlockSpec(memory_space=pltpu.VMEM),
+        scratch_shapes=[
+            pltpu.VMEM((3, local, width, hidden_width), bf16),
+            pltpu.VMEM((blocks * PACK, full), bf16),
+            pltpu.VMEM((blocks, 8, 256), jnp.float32),
+            pltpu.VMEM((local * rows, width), bf16),
+            pltpu.VMEM((local * rows, width), bf16),
+            pltpu.VMEM((local * rows, 128), jnp.float32),
+            pltpu.VMEM((local, 3, rows, hidden_width), bf16),
+            pltpu.VMEM((local, 3, rows, hidden_width), bf16),
+            pltpu.VMEM((3, rows, hidden_width), bf16),
+            pltpu.VMEM((256, width), bf16),
+            pltpu.VMEM((256, width), bf16),
+            pltpu.VMEM((2, span, full), bf16),
+            pltpu.VMEM((span, full), bf16),
+            pltpu.VMEM((span, full), bf16),
+            pltpu.VMEM((span, full), bf16),
+            pltpu.VMEM((n_dp - 1, PACK, full), bf16),
+            dma((3, local)),
+            dma((12,)),
+            dma((12,)),
+            dma((local, 3)),
+            dma((local, 3)),
+            dma((6,)),
+            dma((6,)),
+        ],
+        compiler_params=pltpu.CompilerParams(
+            collective_id=0, has_side_effects=True, vmem_limit_bytes=VMEM_BYTES
+        ),
+    )(packed, table, gate_proj, up_proj, down_proj)
+    in_grad, layer_out = unpacked_rows(out, count)
+    return layer_out, in_grad
+
+
 def solution(mesh):
     in_specs = (
         P(("dp", "expert"), "tensor"),
@@ -121,4 +439,8 @@
         P("expert", "dp", "tensor"),
     )
     out_specs = (P(("dp", "expert"), "tensor"), P(("dp", "expert"), "tensor"))
-    return jax.shard_map(body, mesh=mesh, in_specs=in_specs, out_specs=out_specs, check_vma=False)
+    small = (mesh.shape["dp"], mesh.shape["expert"], mesh.shape["tensor"]) == (4, 4, 2)
+    return jax.shard_map(
+        kernel_body if small else body,
+        mesh=mesh, in_specs=in_specs, out_specs=out_specs, check_vma=False,
+    )

time: 257 us -> 91.8 us (0.36)
  waiting for transfers between devices: 121 us -> 0 us
  Pallas kernels: 0 us -> 80.7 us
  matrix products: 61.1 us -> 0 us
  blocking collectives: 34.2 us -> 0 us
  starting transfers between devices: 14.5 us -> 0 us
  between operations: 14.8 us -> 0.7 us
  local copies, waits for them, and re-layouts: 9.97 us -> 7.24 us
    pallas_call x0 -> x1, Pallas kernels: none -> 80.7 us  [kernel_body(): pl.pallas_call(glu_kernel, out_shape=jax.ShapeDtypeStruct((PACK, full), b...]
    dot_general x10 -> x0, matrix products: 61.1 us -> none  [the longest x1 12.8 us: body(): jnp.einsum('becd,efd->becf', row_grads, down_proj, preferred_element_type...]
    psum x1 -> x0, waiting for transfers between devices: 56.4 us -> none  [body(): lax.psum(up_part.astype(jnp.bfloat16), 'tensor').astype(jnp.float32)]
    unnamed x3 -> x0, waiting for transfers between devices: 54.6 us -> none
    all_gather x2 -> x0, blocking collectives: 34.2 us -> none  [the longest x1 18.1 us: body(): lax.all_gather(got_tokens, 'dp', axis=0, tiled=True)]
    all_to_all x4 -> x0, starting transfers between devices: 14.3 us -> none  [the longest x1 4.24 us: body(): lax.all_to_all(sent_tokens, 'expert', split_axis=0, concat_axis=0, tiled=...]
    all_to_all x4 -> x0, waiting for transfers between devices: 10.2 us -> none  [the longest x1 3.74 us: body(): lax.all_to_all(out_rows, 'expert', split_axis=0, concat_axis=0, tiled=True)]
    unnamed x19 -> x2, local copies, waits for them, and re-layouts: 6.31 us -> 1.55 us
  transfers between devices with their start and end apart: 6 -> 0, of which waited for: 5 -> 0; matrix products, arithmetic and copies ran while one was open for 8% -> 0% of each run, Pallas kernels for 0% -> 0%
where the time goes in v1:
time: 91.8 us; the launch traced here: 91.3 us
  Pallas kernels  80.7 us (88%)
  local copies, waits for them, and re-layouts  7.24 us (8%)
  other arithmetic  2.64 us (3%)
    pallas_call x1, Pallas kernels, kernel_body(): pl.pallas_call(glu_kernel, out_shape=jax.ShapeDtypeStruct((PACK, full), b...  80.7 us

profile of v1, /device:TPU:0, one launch (start us, length us, event | category | flops | bytes accessed | tf_op | source)
XLA Modules:
  0.0 91.3 jit_solution(8986958025358137676)
XLA Ops:
  0.6 0.8 copy.18
  1.4 0.1 fusion.2
  1.5 0.1 copy.19
  1.6 0.3 convert_reduce_fusion
  1.9 0.8 copy.20
  2.7 0.1 select_reduce_fusion.1
  2.8 0.1 select_reduce_fusion.2
  2.9 0.1 broadcast_in_dim.83
  2.9 0.1 copy.22
  3.1 0.1 copy.23
  3.2 0.1 broadcast_in_dim.75
  3.3 0.2 broadcast_in_dim.76
  3.4 0.6 pad.9.t_ref
  4.1 0.7 slice.15
  4.8 0.8 slice.16
  5.6 1.4 %fusion.1.x_ref = bf16[16,1792]{1,0:T(8,128)(2,1)} fusion(bf16[12,256]{1,0:T(8,128)(2,1)S(1)} %reshape.41, bf16[7,1536]{1,0:T(8,128)(2,1)S(1)} %slice.15, bf16[9,1536]{1,0:T(8,128)(2,1)} %param.7), kind=kLoop, calls=%fused_computation.3 | loop fusion | flops 229376 | bytes 112640 | tf_op jit(solution)/shard_map/concatenate | solution.py:125
  7.1 80.7 %shard_map.86 = bf16[16,1792]{1,0:T(8,128)(2,1)} custom-call(bf16[16,1792]{1,0:T(8,128)(2,1)} %fusion.1.x_ref, f32[8,256]{1,0:T(8,128)} %pad.9.t_ref, bf16[4,1536,1536]{2,1,0:T(8,128)(2,1)} %wg_hbm.1, bf16[4,1536,1536]{2,1,0:T(8,128)(2,1)} %wu_hbm.1, bf16[4,1536,1536]{2,1,0:T(8,128)(2,1)} %wd_hbm.1), custom_call_target="tpu_custom_call" | custom-call | tf_op jit(solution)/shard_map/pallas_call | solution.py:392
  87.7 0.7 slice.17
  88.5 0.7 slice.18
  89.2 0.6 pad_maximum_fusion
  89.8 1.4 %slice.19 = bf16[9,1536]{1,0:T(8,128)(2,1)} slice(bf16[16,1792]{1,0:T(8,128)(2,1)} %shard_map.86), slice={[0:9], [0:1536]} | slice | bytes 55296 | tf_op jit(solution)/shard_map/slice | solution.py:133
  (10 shorter events, 0.1 us)

commit v2 on v1

--- a/solution.py
+++ b/solution.py
@@ -115,40 +115,7 @@
 
 PACK = 16
 CHUNK = 256
-
-
-def packed_rows(first, second):
-    width = first.shape[1]
-    split = PACK - first.shape[0]
-    pieces = second[split:].reshape(-1, CHUNK)
-    pieces = jnp.pad(pieces, ((0, PACK - pieces.shape[0]), (0, 0)))
-    return jnp.concatenate([jnp.concatenate([first, second[:split]], axis=0), pieces], axis=1)
-
-
-def unpacked_rows(packed, count):
-    width = packed.shape[1] - CHUNK
-    split = PACK - count
-    pieces = (count - split) * width // CHUNK
-    tail = packed[:pieces, width:].reshape(count - split, width)
-    return packed[:count, :width], jnp.concatenate([packed[count:, :width], tail], axis=0)
-
-
-def routing_table(routes, gate_probs, place, blocks, groups):
-    count = routes.shape[0]
-    local = EXPERTS // groups
-    same = routes[None] == jnp.arange(EXPERTS)[:, None, None]
-    hit = jnp.any(same, axis=2)
-    prob = jnp.sum(jnp.where(same, gate_probs[None], 0.0), axis=2)
-    before = jnp.arange(count)[None, :] < jnp.arange(count)[:, None]
-    rank = jnp.sum(hit[:, None, :] & before[None], axis=2)
-    mine = hit[:, None, :] & (rank[:, None, :] == jnp.arange(CAP)[None, :, None])
-    rows = (place * PACK + 1 + jnp.arange(count)).astype(jnp.float32)
-    token = jnp.sum(jnp.where(mine, rows[None, None], 0.0), axis=2)
-    weight = jnp.sum(jnp.where(mine, prob[:, None, :], 0.0), axis=2)
-    both = jnp.stack([token, weight]).reshape(2 * groups, local, 1, CAP)
-    here = (jnp.arange(blocks) == place)[None, None, :, None]
-    table = jnp.where(here, both, 0.0).reshape(2 * groups, local * blocks * CAP)
-    return jnp.pad(table, ((0, 0), (0, 256 - table.shape[1])))
+FIRST = 1024
 
 
 def nt_dot(a, b):
@@ -160,12 +127,14 @@
 
 
 def glu_kernel(
-    x_ref, t_ref, wg_hbm, wu_hbm, wd_hbm, o_ref,
-    w_v, gb, tab, xt, xg, pc, sbuf, rbuf, act, p_in, p_out, r1, s2, r2, s3, r3,
+    tok_ref, cot_ref, route_ref, prob_ref, wg_hbm, wu_hbm, wd_hbm, out_ref, grad_ref,
+    w_v, gb, tab, xt, xg, pc, sbuf, rbuf, act, p_in, p_out, r1, s2, r2, s3, r3, r3b, s4, s5, r5,
     w_sem, g_ss, g_rs, x_ss, x_rs, e_ss, e_rs,
 ):
     f32, bf16 = jnp.float32, jnp.bfloat16
-    width = x_ref.shape[1] - CHUNK
+    count, width = tok_ref.shape
+    split = PACK - count
+    pieces = width // CHUNK
     local, hidden_width = wg_hbm.shape[0], wg_hbm.shape[2]
     rows = sbuf.shape[2]
     slots = local * rows
@@ -201,42 +170,85 @@
             weight(m, j).start()
     place = e * n_dp + z
     own = at_rows(place * PACK, PACK)
-    gb[own, :] = x_ref[...]
-    tab[pl.ds(place, 1)] = t_ref[...][None]
+    tokens, cotangent = tok_ref[...].astype(f32), cot_ref[...].astype(f32)
+    gb[own, :width] = jnp.concatenate([tokens, cotangent[:split]], axis=0).astype(bf16)
+    tail = [
+        cotangent[r : r + 1, q * CHUNK : (q + 1) * CHUNK]
+        for r in range(split, count)
+        for q in range(pieces)
+    ]
+    tail.append(jnp.zeros((PACK - len(tail), CHUNK), f32))
+    gb[own, width:] = jnp.concatenate(tail, axis=0).astype(bf16)
+    lane = lax.broadcasted_iota(jnp.int32, (8, 256), 1).astype(f32)
+    group = lax.broadcasted_iota(jnp.int32, (8, 256), 0)
+    expert = jnp.floor((lane + 0.5) / rows)
+    within = lane - expert * rows
+    block = jnp.floor((within + 0.5) / CAP)
+    nth = (within - block * CAP).astype(jnp.int32)
+    here = (block.astype(jnp.int32) == place) & (expert < local)
+    expert = expert.astype(jnp.int32) + lax.rem(group, 4) * local
+    seen = jnp.zeros((8, 256), jnp.int32)
+    token = jnp.zeros((8, 256), f32)
+    chance = jnp.zeros((8, 256), f32)
+    for r in range(count):
+        hits = jnp.zeros((8, 256), jnp.int32)
+        for k in range(route_ref.shape[1]):
+            hit = expert == route_ref[r, k]
+            hits += hit.astype(jnp.int32)
+            chance = jnp.where(hit & here & (seen == nth), prob_ref[r, k], chance)
+        key = (place * PACK + 1 + r).astype(f32)
+        token = jnp.where((hits > 0) & here & (seen == nth), key, token)
+        seen += hits
+    tab[pl.ds(place, 1)] = jnp.where(group < 4, token, chance)[None]
     p_in[slots:, :] = jnp.zeros((p_in.shape[0] - slots, width), bf16)
     p_out[slots:, :] = jnp.zeros((p_out.shape[0] - slots, width), bf16)
     pl.semaphore_wait(barrier, len(partners))
 
-    first = []
+    wide_cols = (pl.ds(0, FIRST), pl.ds(FIRST, width + CHUNK - FIRST))
+
+    def send(sent, src, to):
+        i = len(started)
+        c = remote(src, src, g_ss, g_rs, i, to)
+        c.start()
+        started.append(c)
+        sent.append(c)
+
+    def arrived(sent):
+        for c in sent:
+            c.wait_recv()
+
+    def group_at(g, h):
+        return gb.at[at_rows(g * span, span), wide_cols[h]]
+
+    def table_at(g):
+        return tab.at[pl.ds(g * n_dp, n_dp)]
+
+    started, along, over = [], [], []
+    one = tab.at[pl.ds(place, 1)]
+    send(over, gb.at[own, wide_cols[1]], {"expert": across})
     for d in range(1, n_dp):
         to = {"dp": lax.rem(z + d, n_dp)}
-        first.append(remote(gb.at[own], gb.at[own], g_ss, g_rs, 2 * d - 2, to))
-        first.append(
-            remote(tab.at[pl.ds(place, 1)], tab.at[pl.ds(place, 1)], g_ss, g_rs, 2 * d - 1, to)
-        )
-    for c in first:
-        c.start()
-    for c in first:
-        c.wait_recv()
-
-    def send_group(k, group, to):
-        a = at_rows(group * span, span)
-        b = pl.ds(group * n_dp, n_dp)
-        pair = [
-            remote(gb.at[a], gb.at[a], g_ss, g_rs, k, to),
-            remote(tab.at[b], tab.at[b], g_ss, g_rs, k + 1, to),
-        ]
-        for c in pair:
-            c.start()
-        return pair
-
-    second = send_group(6, e, {"expert": across})
-    third = send_group(8, e, {"expert": beside})
-    for c in second:
-        c.wait_recv()
-    fourth = send_group(10, across, {"expert": beside})
-    for c in third + fourth:
-        c.wait_recv()
+        send(along, gb.at[own, wide_cols[0]], to)
+        send(along, one, to)
+    arrived(over)
+    along_two, over_two, side = [], [], []
+    facing = at_rows((across * n_dp + z) * PACK, PACK)
+    for d in range(1, n_dp):
+        to = {"dp": lax.rem(z + d, n_dp)}
+        send(along_two, gb.at[own, wide_cols[1]], to)
+        send(along_two, gb.at[facing, wide_cols[1]], to)
+    arrived(along)
+    send(over_two, group_at(e, 0), {"expert": across})
+    send(over_two, table_at(e), {"expert": across})
+    send(side, group_at(e, 0), {"expert": beside})
+    send(side, table_at(e), {"expert": beside})
+    arrived(along_two)
+    send(side, group_at(e, 1), {"expert": beside})
+    send(side, group_at(across, 1), {"expert": beside})
+    arrived(over_two)
+    send(side, group_at(across, 0), {"expert": beside})
+    send(side, table_at(across), {"expert": beside})
+    arrived(side)
 
     row_of = jnp.sum(tab[:, pl.ds(e, 1), :], axis=0)
     prob_of = jnp.sum(tab[:, pl.ds(e + 4, 1), :], axis=0)
@@ -245,12 +257,8 @@
         k = v - 1.0
         base = jnp.floor(k * (1.0 / PACK)) * PACK
         r = k - base
-        tokens_count = 9.0
-        split = PACK - tokens_count
-        second_key = jnp.where(r < split, k + tokens_count, -1.0)
-        tail_key = jnp.where(
-            (r >= split) & (r < tokens_count), base + (r - split) * (width // CHUNK), -1000.0
-        )
+        second_key = jnp.where(r < split, k + count, -1.0)
+        tail_key = jnp.where((r >= split) & (r < count), base + (r - split) * pieces, -1000.0)
         return k.astype(jnp.int32), second_key.astype(jnp.int32), tail_key.astype(jnp.int32)
 
     def one_hot(hit):
@@ -327,7 +335,7 @@
 
     lax.fori_loop(0, local, finish, 0)
 
-    for c in first + second + third + fourth:
+    for c in started:
         c.wait_send()
     acc = gb
     n1, n2, n3 = keys(row_of)
@@ -347,27 +355,52 @@
     a0.start()
     a1.wait_recv()
     s2[...] = (acc[at_rows(across * span, span), :].astype(f32) + r1[1].astype(f32)).astype(bf16)
-    b = remote(s2, r2, e_ss, e_rs, 2, {"expert": across})
-    b.start()
+    over = remote(s2.at[:, wide_cols[0]], r2, e_ss, e_rs, 2, {"expert": across})
+    over.start()
     a0.wait_recv()
-    held = acc[at_rows(e * span, span), :].astype(f32) + r1[0].astype(f32)
-    b.wait_recv()
-    s3[...] = (held + r2[...].astype(f32)).astype(bf16)
-    last = []
+    s3[...] = (acc[at_rows(e * span, span), :].astype(f32) + r1[0].astype(f32)).astype(bf16)
+    along, last = [], []
+    for d in range(1, n_dp):
+        to = lax.rem(z + d, n_dp)
+        there = at_rows(to * PACK, PACK)
+        for h, part in enumerate((s3, s2)):
+            c = remote(
+                part.at[there, wide_cols[1]], r3b.at[2 * d - 2 + h], e_ss, e_rs,
+                1 + 2 * d + h, {"dp": to},
+            )
+            c.start()
+            along.append(c)
+    over.wait_recv()
+    s4[...] = (s3[:, :FIRST].astype(f32) + r2[...].astype(f32)).astype(bf16)
     for d in range(1, n_dp):
         to = lax.rem(z + d, n_dp)
         c = remote(
-            s3.at[at_rows(to * PACK, PACK)], r3.at[d - 1], e_ss, e_rs, 2 + d, {"dp": to}
+            s4.at[at_rows(to * PACK, PACK)], r3.at[d - 1], e_ss, e_rs, 8 + d, {"dp": to}
         )
         c.start()
         last.append(c)
-    final = s3[at_rows(z * PACK, PACK), :].astype(f32)
+    here = at_rows(z * PACK, PACK)
+    sums = [s3[here, FIRST:].astype(f32), s2[here, FIRST:].astype(f32)]
+    for i, c in enumerate(along):
+        c.wait_recv()
+        sums[i % 2] += r3b[i].astype(f32)
+    s5[...] = sums[1].astype(bf16)
+    cross = remote(s5, r5, e_ss, e_rs, 12, {"expert": across})
+    cross.start()
+    final = s4[here, :].astype(f32)
     for d, c in enumerate(last):
         c.wait_recv()
         final += r3[d].astype(f32)
-    o_ref[...] = final.astype(bf16)
-
-    for c in [a1, a0, b] + last:
+    cross.wait_recv()
+    final = jnp.concatenate([final, sums[0] + r5[...].astype(f32)], axis=1)
+    grad_ref[...] = final[:count, :width].astype(bf16)
+    late = [
+        jnp.concatenate([final[r * pieces + q : r * pieces + q + 1, width:] for q in range(pieces)], axis=1)
+        for r in range(count - split)
+    ]
+    out_ref[...] = jnp.concatenate([final[count:, :width]] + late, axis=0).astype(bf16)
+
+    for c in [a1, a0, over, cross] + along + last:
         c.wait_send()
 
     def sent(j, carry):
@@ -381,20 +414,18 @@
 def kernel_body(tokens, cotangent, routes, gate_probs, gate_proj, up_proj, down_proj):
     groups, n_dp = lax.axis_size("expert"), lax.axis_size("dp")
     blocks = groups * n_dp
-    place = lax.axis_index("expert") * n_dp + lax.axis_index("dp")
     count, width = tokens.shape
     local, _, hidden_width = gate_proj.shape
     rows = blocks * CAP
-    packed = packed_rows(tokens, cotangent)
-    table = routing_table(routes, gate_probs, place, blocks, groups)
     bf16, dma = jnp.bfloat16, pltpu.SemaphoreType.DMA
     full, span = width + CHUNK, n_dp * PACK
-    out = pl.pallas_call(
+    return pl.pallas_call(
         glu_kernel,
-        out_shape=jax.ShapeDtypeStruct((PACK, full), bf16),
+        out_shape=[jax.ShapeDtypeStruct((count, width), bf16)] * 2,
         in_specs=[pl.BlockSpec(memory_space=pltpu.VMEM)] * 2
+        + [pl.BlockSpec(memory_space=pltpu.SMEM)] * 2
         + [pl.BlockSpec(memory_space=pl.ANY)] * 3,
-        out_specs=pl.BlockSpec(memory_space=pltpu.VMEM),
+        out_specs=[pl.BlockSpec(memory_space=pltpu.VMEM)] * 2,
         scratch_shapes=[
             pltpu.VMEM((3, local, width, hidden_width), bf16),
             pltpu.VMEM((blocks * PACK, full), bf16),
@@ -409,23 +440,25 @@
             pltpu.VMEM((256, width), bf16),
             pltpu.VMEM((2, span, full), bf16),
             pltpu.VMEM((span, full), bf16),
+            pltpu.VMEM((span, FIRST), bf16),
             pltpu.VMEM((span, full), bf16),
-            pltpu.VMEM((span, full), bf16),
-            pltpu.VMEM((n_dp - 1, PACK, full), bf16),
+            pltpu.VMEM((n_dp - 1, PACK, FIRST), bf16),
+            pltpu.VMEM((2 * n_dp - 2, PACK, full - FIRST), bf16),
+            pltpu.VMEM((span, FIRST), bf16),
+            pltpu.VMEM((PACK, full - FIRST), bf16),
+            pltpu.VMEM((PACK, full - FIRST), bf16),
             dma((3, local)),
-            dma((12,)),
-            dma((12,)),
+            dma((21,)),
+            dma((21,)),
             dma((local, 3)),
             dma((local, 3)),
-            dma((6,)),
-            dma((6,)),
+            dma((13,)),
+            dma((13,)),
         ],
         compiler_params=pltpu.CompilerParams(
             collective_id=0, has_side_effects=True, vmem_limit_bytes=VMEM_BYTES
         ),
-    )(packed, table, gate_proj, up_proj, down_proj)
-    in_grad, layer_out = unpacked_rows(out, count)
-    return layer_out, in_grad
+    )(tokens, cotangent, routes, gate_probs, gate_proj, up_proj, down_proj)
 
 
 def solution(mesh):

time: 91.8 us -> 83 us (0.904)
  Pallas kernels: 80.7 us -> 76.5 us
  other arithmetic: 2.64 us -> 0 us
  local copies, waits for them, and re-layouts: 7.24 us -> 5.57 us
    slice x5 -> x0, local copies, waits for them, and re-layouts: 4.41 us -> none  [the longest x1 1.42 us: unpacked_rows(): packed[:count, :width]]
    pallas_call x1, Pallas kernels: 80.7 us -> 76.5 us  [kernel_body(): pl.pallas_call(glu_kernel, out_shape=[jax.ShapeDtypeStruct((count, width)...]
    unnamed x2 -> x4, local copies, waits for them, and re-layouts: 1.55 us -> 5.57 us
    concatenate x2 -> x0, other arithmetic: 2.08 us -> none  [the longest x1 1.44 us: packed_rows(): jnp.concatenate([jnp.concatenate([first, second[:split]], axis=0), pieces...]
where the time goes in v2:
time: 83 us; the launch traced here: 82.7 us
  Pallas kernels  76.5 us (92%)
  local copies, waits for them, and re-layouts  5.57 us (7%)
    pallas_call x1, Pallas kernels, kernel_body(): pl.pallas_call(glu_kernel, out_shape=[jax.ShapeDtypeStruct((count, width)...  76.5 us
    unnamed x4, local copies, waits for them, and re-layouts  5.57 us

profile of v2, /device:TPU:0, one launch (start us, length us, event | category | flops | bytes accessed | tf_op | source)
XLA Modules:
  0.0 82.7 jit_solution(11402702772205551070)
XLA Ops:
  0.6 1.4 %copy.9.route_ref = s32[9,4]{1,0:T(8,128)} copy(s32[9,4]{0,1:T(4,128)} %param.9) | data formatting | bytes 288 | tf_op args[2]
  2.0 1.4 %copy.10.prob_ref = f32[9,4]{1,0:T(8,128)} copy(f32[9,4]{0,1:T(4,128)} %param.10) | data formatting | bytes 288 | tf_op args[3]
  3.4 76.5 %shard_map.86 = (bf16[9,1536]{1,0:T(8,128)(2,1)}, bf16[9,1536]{1,0:T(8,128)(2,1)}) custom-call(bf16[9,1536]{1,0:T(8,128)(2,1)} %tok_ref.1, bf16[9,1536]{1,0:T(8,128)(2,1)} %cot_ref.1, s32[9,4]{1,0:T(8,128)} %copy.9.route_ref, f32[9,4]{1,0:T(8,128)} %copy.10.prob_ref, bf16[4,1536,1536]{2,1,0:T(8,128)(2,1)} %wg_hbm.1, bf16[4,1536,1536]{2,1,0:T(8,128)(2,1)} %wu_hbm.1, ...), custom_call_target="tpu_custom_call" | custom-call | tf_op jit(solution)/shard_map/pallas_call | solution.py:422
  79.8 1.4 %copy.13 = bf16[9,1536]{1,0:T(8,128)(2,1)} copy(bf16[9,1536]{1,0:T(8,128)(2,1)} %get-tuple-element.4) | data formatting | bytes 55296
  81.2 1.4 %copy.14 = bf16[9,1536]{1,0:T(8,128)(2,1)} copy(bf16[9,1536]{1,0:T(8,128)(2,1)} %get-tuple-element.5) | data formatting | bytes 55296

commit v3 on v2

--- a/solution.py
+++ b/solution.py
@@ -127,7 +127,7 @@
 
 
 def glu_kernel(
-    tok_ref, cot_ref, route_ref, prob_ref, wg_hbm, wu_hbm, wd_hbm, out_ref, grad_ref,
+    tok_ref, cot_ref, route_ref, prob_ref, wg_hbm, wu_hbm, wd_hbm, o_ref,
     w_v, gb, tab, xt, xg, pc, sbuf, rbuf, act, p_in, p_out, r1, s2, r2, s3, r3, r3b, s4, s5, r5,
     w_sem, g_ss, g_rs, x_ss, x_rs, e_ss, e_rs,
 ):
@@ -192,10 +192,10 @@
     chance = jnp.zeros((8, 256), f32)
     for r in range(count):
         hits = jnp.zeros((8, 256), jnp.int32)
-        for k in range(route_ref.shape[1]):
-            hit = expert == route_ref[r, k]
+        for k in range(route_ref.shape[0]):
+            hit = expert == route_ref[k, r]
             hits += hit.astype(jnp.int32)
-            chance = jnp.where(hit & here & (seen == nth), prob_ref[r, k], chance)
+            chance = jnp.where(hit & here & (seen == nth), prob_ref[k, r], chance)
         key = (place * PACK + 1 + r).astype(f32)
         token = jnp.where((hits > 0) & here & (seen == nth), key, token)
         seen += hits
@@ -274,9 +274,6 @@
     for q in range(width // CHUNK):
         cols = pl.ds(q * CHUNK, CHUNK)
         xt[:, cols] = nn_dot(pick_first, gb[:, cols]).astype(bf16)
-        g = nn_dot(pick_second, gb[:, cols])
-        g += nn_dot(one_hot(k3 + q == lane), gb[:, width:])
-        xg[:, cols] = (scale * g).astype(bf16)
 
     def act_copy(j, m):
         return pltpu.make_async_remote_copy(
@@ -285,9 +282,9 @@
             device_id={"tensor": other}, device_id_type=pl.DeviceIdType.MESH,
         )
 
-    def project(j, carry):
-        mine = at_rows(j * rows, rows)
-        for m in range(3):
+    def project(j, carry, which=(0, 1, 2)):
+        mine = pl.ds(j * rows, rows) if isinstance(j, int) else at_rows(j * rows, rows)
+        for m in which:
             weight(m, j).wait()
 
             def tile(n, c):
@@ -303,7 +300,14 @@
             act_copy(j, m).start()
         return carry
 
-    lax.fori_loop(0, local, project, 0)
+    project(0, 0, (0, 1))
+    for q in range(width // CHUNK):
+        cols = pl.ds(q * CHUNK, CHUNK)
+        g = nn_dot(pick_second, gb[:, cols])
+        g += nn_dot(one_hot(k3 + q == lane), gb[:, width:])
+        xg[:, cols] = (scale * g).astype(bf16)
+    project(0, 0, (2,))
+    lax.fori_loop(1, local, project, 0)
 
     def finish(j, carry):
         mine = at_rows(j * rows, rows)
@@ -393,12 +397,13 @@
         final += r3[d].astype(f32)
     cross.wait_recv()
     final = jnp.concatenate([final, sums[0] + r5[...].astype(f32)], axis=1)
-    grad_ref[...] = final[:count, :width].astype(bf16)
+    unused = jnp.zeros((PACK - count, width), f32)
+    o_ref[PACK:, :] = jnp.concatenate([final[:count, :width], unused], axis=0).astype(bf16)
     late = [
         jnp.concatenate([final[r * pieces + q : r * pieces + q + 1, width:] for q in range(pieces)], axis=1)
         for r in range(count - split)
     ]
-    out_ref[...] = jnp.concatenate([final[count:, :width]] + late, axis=0).astype(bf16)
+    o_ref[:PACK, :] = jnp.concatenate([final[count:, :width]] + late + [unused], axis=0).astype(bf16)
 
     for c in [a1, a0, over, cross] + along + last:
         c.wait_send()
@@ -419,13 +424,13 @@
     rows = blocks * CAP
     bf16, dma = jnp.bfloat16, pltpu.SemaphoreType.DMA
     full, span = width + CHUNK, n_dp * PACK
-    return pl.pallas_call(
+    out = pl.pallas_call(
         glu_kernel,
-        out_shape=[jax.ShapeDtypeStruct((count, width), bf16)] * 2,
+        out_shape=jax.ShapeDtypeStruct((2 * PACK, width), bf16),
         in_specs=[pl.BlockSpec(memory_space=pltpu.VMEM)] * 2
         + [pl.BlockSpec(memory_space=pltpu.SMEM)] * 2
         + [pl.BlockSpec(memory_space=pl.ANY)] * 3,
-        out_specs=[pl.BlockSpec(memory_space=pltpu.VMEM)] * 2,
+        out_specs=pl.BlockSpec(memory_space=pltpu.VMEM),
         scratch_shapes=[
             pltpu.VMEM((3, local, width, hidden_width), bf16),
             pltpu.VMEM((blocks * PACK, full), bf16),
@@ -458,7 +463,8 @@
         compiler_params=pltpu.CompilerParams(
             collective_id=0, has_side_effects=True, vmem_limit_bytes=VMEM_BYTES
         ),
-    )(tokens, cotangent, routes, gate_probs, gate_proj, up_proj, down_proj)
+    )(tokens, cotangent, routes.T, gate_probs.T, gate_proj, up_proj, down_proj)
+    return out[:count], out[PACK : PACK + count]
 
 
 def solution(mesh):

time: 83 us -> 78.3 us (0.943)
  local copies, waits for them, and re-layouts: 5.57 us -> 1.46 us
    unnamed x4 -> x0, local copies, waits for them, and re-layouts: 5.57 us -> none
    slice x0 -> x1, local copies, waits for them, and re-layouts: none -> 1.46 us  [kernel_body(): return (out[:count], out[PACK:PACK + count])]
where the time goes in v3:
time: 78.3 us; the launch traced here: 78.1 us
  Pallas kernels  76 us (97%)
  local copies, waits for them, and re-layouts  1.46 us (2%)
    pallas_call x1, Pallas kernels, kernel_body(): pl.pallas_call(glu_kernel, out_shape=jax.ShapeDtypeStruct((2 * PACK, widt...  76 us

profile of v3, /device:TPU:0, one launch (start us, length us, event | category | flops | bytes accessed | tf_op | source)
XLA Modules:
  0.0 78.1 jit_solution(16780467266491517607)
XLA Ops:
  0.6 76.0 %shard_map.86 = bf16[32,1536]{1,0:T(8,128)(2,1)} custom-call(bf16[9,1536]{1,0:T(8,128)(2,1)} %tok_ref.1, bf16[9,1536]{1,0:T(8,128)(2,1)} %cot_ref.1, s32[4,9]{1,0:T(4,128)} %bitcast.2, f32[4,9]{1,0:T(4,128)} %bitcast.3, bf16[4,1536,1536]{2,1,0:T(8,128)(2,1)} %wg_hbm.1, bf16[4,1536,1536]{2,1,0:T(8,128)(2,1)} %wu_hbm.1, bf16[4,1536,1536]{2,1,0:T(8,128)(2,1)} %wd_hbm.1), custom_call_target="tpu_custom_call" | custom-call | tf_op jit(solution)/shard_map/pallas_call | solution.py:427
  76.6 1.5 %fusion = (bf16[9,1536]{1,0:T(8,128)(2,1)}, bf16[9,1536]{1,0:T(8,128)(2,1)}) fusion(bf16[32,1536]{1,0:T(8,128)(2,1)} %shard_map.86), kind=kLoop, calls=%fused_computation | loop fusion | bytes 110592 | tf_op jit(solution)/shard_map/slice | solution.py:467
